TPU v7x, 128 devices: a whole 4x4x4 slice. The times are simulated.
128 devices in a mesh: layer: 2 (over core), feat: 64 (over y, x, z).
Axes of the slice: x: 4, y: 4, z: 4, core: 2. Of those that a mesh axis runs over, the one named last changes fastest.
Arguments:
- inputs: bfloat16 [2, 512, 4608], P('layer', 'feat'), may hold values from -6 to 6
- targets: bfloat16 [2, 512, 4608], P('layer', 'feat'), may hold values from -6 to 6
- w_enc: bfloat16 [2, 4608, 32768], P('layer', None, 'feat'), may hold values from -0.09375 to 0.09375
- b_enc: float32 [2, 32768], P('layer', 'feat'), may hold values from -4 to 4
- w_self: bfloat16 [2, 32768, 4608], P('layer', 'feat'), may hold values from -0.1875 to 0.1875
- w_cross: bfloat16 [32768, 4608], P('feat', 'layer'), may hold values from -0.1875 to 0.1875
- block_ids: int32 [2, 512, 8], P('layer', 'feat'), may hold values from 0 to 255, all different within a row
Outputs:
- reconstruction: float32 [2, 512, 4608], P('layer', 'feat')
- active_codes: bfloat16 [2, 512, 8, 128], P('layer', 'feat')
- grad_enc: bfloat16 [2, 4608, 32768], P('layer', None, 'feat')
- grad_benc: float32 [2, 32768], P('layer', 'feat')
- grad_self: bfloat16 [2, 32768, 4608], P('layer', 'feat')
- grad_cross: bfloat16 [32768, 4608], P('feat', 'layer')
Inputs may be any that keep to these rules, and one draw needn't show every extreme that they name: `block_ids`: each token names 8 different blocks in each layer; every block is named by some token of the two layers taken together.
All inputs are finite; a program needn't handle non-finite values.
Results may differ from a plain program's by a relative error of at most 0.0058.
Values may be sent and summed in bfloat16 or wider, within the bound.
No kernel may reach another device: no remote copies, remote signals or barrier semaphores. Data moves between devices by JAX's collectives and lax.ppermute only.
A program may use at most 128 MiB of HBM per device.

v0:
```python
import jax
import jax.numpy as jnp
from jax import lax
from jax.sharding import PartitionSpec as P

BLK = 128


def shifted(block, axis, distance):
    devices = range(lax.axis_size(axis))
    route = [(i - distance, i) for i in devices if i - distance in devices]
    return lax.ppermute(block, axis, route)


def contract_rows(left, right):
    return lax.dot_general(
        left, right, (((0,), (0,)), ((), ())), preferred_element_type=jnp.float32
    )


def contract_cols(left, right):
    return lax.dot_general(
        left, right, (((1,), (1,)), ((), ())), preferred_element_type=jnp.float32
    )


def per_device(inputs, targets, w_enc, b_enc, w_self, w_cross, block_ids):
    layer_index = lax.axis_index("layer")
    shard_index = lax.axis_index("feat")
    first_layer = layer_index == 0
    own_rows = inputs[0]
    token_rows = own_rows.shape[0]
    model_width = own_rows.shape[1]
    half_width = model_width // 2
    latent_dev = w_enc.shape[2]
    blocks_dev = latent_dev // BLK
    block_count = blocks_dev * lax.axis_size("feat")
    token_blocks = block_ids[0]
    numbers = jnp.arange(block_count, dtype=jnp.int32)
    block_table = jnp.any(token_blocks[:, :, None] == numbers[None, None, :], axis=1).astype(
        jnp.bfloat16
    )
    whole_rows, whole_table = (
        lax.all_gather(own_rows, "feat", axis=0, tiled=True),
        lax.all_gather(block_table, "feat", axis=0, tiled=True),
    )
    local_table = lax.dynamic_slice_in_dim(whole_table, shard_index * blocks_dev, blocks_dev, 1)
    active = jnp.repeat(local_table.astype(jnp.float32), BLK, axis=1)
    pre_acts = jnp.dot(whole_rows, w_enc[0], preferred_element_type=jnp.float32) + b_enc[0]
    latent_codes = (active * jax.nn.softplus(pre_acts)).astype(jnp.bfloat16)
    earlier = shifted(latent_codes, "layer", 1)
    source = jnp.where(first_layer, latent_codes, earlier)
    cross_part = jnp.dot(source, w_cross, preferred_element_type=jnp.float32)
    self_part = jnp.dot(latent_codes, w_self[0], preferred_element_type=jnp.float32)
    padded = jnp.concatenate([jnp.zeros_like(cross_part), cross_part], axis=1)
    main_term = self_part + jnp.where(first_layer, 0.0, padded)
    outgoing = jnp.where(first_layer, cross_part, 0.0)
    rows_main, rows_cross = (
        lax.psum_scatter(main_term, "feat", scatter_dimension=0, tiled=True),
        lax.psum_scatter(outgoing, "feat", scatter_dimension=0, tiled=True),
    )
    moved_rows = shifted(rows_cross, "layer", 1)
    recon_rows = rows_main + jnp.concatenate([moved_rows, jnp.zeros_like(moved_rows)], axis=1)
    errors_own = (recon_rows - targets[0].astype(jnp.float32)).astype(jnp.bfloat16)
    errors = lax.all_gather(errors_own, "feat", axis=0, tiled=True)
    returned = shifted(errors[:, :half_width], "layer", -1)
    cross_err = jnp.where(first_layer, returned, errors[:, half_width:])
    grad_self = contract_rows(latent_codes, errors).astype(jnp.bfloat16)
    grad_cross = contract_rows(source, cross_err).astype(jnp.bfloat16)
    self_term = contract_cols(errors, w_self[0])
    cross_term = contract_cols(cross_err, w_cross)
    back_term = shifted(cross_term, "layer", -1)
    code_grads = self_term + jnp.where(first_layer, cross_term + back_term, 0.0)
    pre_grads = (code_grads * active * jax.nn.sigmoid(pre_acts)).astype(jnp.bfloat16)
    grad_enc = contract_rows(whole_rows, pre_grads).astype(jnp.bfloat16)
    grad_benc = jnp.sum(pre_grads.astype(jnp.float32), axis=0)
    arrived_codes = lax.all_to_all(latent_codes, "feat", split_axis=0, concat_axis=1, tiled=True)
    blocks = arrived_codes.reshape(token_rows, block_count, BLK)
    row_index = jnp.arange(token_rows, dtype=jnp.int32)[:, None]
    picked = blocks[row_index, token_blocks]
    return (
        recon_rows[None],
        picked[None],
        grad_enc[None],
        grad_benc[None],
        grad_self[None],
        grad_cross,
    )


def solution(mesh):
    placed = (
        P("layer", "feat", None),
        P("layer", "feat", None),
        P("layer", None, "feat"),
        P("layer", "feat"),
        P("layer", "feat", None),
        P("feat", "layer"),
        P("layer", "feat", None),
    )
    return jax.shard_map(
        per_device,
        mesh=mesh,
        in_specs=placed,
        out_specs=(
            P("layer", "feat", None),
            P("layer", "feat", None, None),
            P("layer", None, "feat"),
            P("layer", "feat"),
            P("layer", "feat", None),
            P("feat", "layer"),
        ),
        check_vma=False,
    )
```

profile of v0, /device:TPU:1, one launch (start us, length us, event | category | flops | bytes accessed | tf_op | source)
XLA Modules:
  0.0 786.4 jit_solution(4449957219626329554)
XLA Ops:
  7.2 0.0 copy-start
  7.2 0.0 all-gather.6.cloned.1.call-start
  7.2 0.7 all-gather.6.cloned.1.call-update
  7.9 0.0 reduce-scatter.5.cloned.1.call-start
  8.0 0.8 fusion.25
  8.8 152.7 %all_gather.9 = bf16[512,256]{1,0:T(8,128)(2,1)S(1)} all-gather(bf16[8,256]{1,0:T(8,128)(2,1)S(1)} %convert_element_type.36), channel_id=1, replica_groups=mesh['layer'=2,'feat'=64] {'feat'}, dimensions={0}, use_global_device_ids=true | all-gather | bytes 266240 | tf_op jit(solution)/shard_map/all_gather | solution.py:45
  161.4 0.1 dynamic-slice_convert_fusion
  161.5 0.0 all-gather.6.cloned.1.call-done
  161.6 0.6 broadcast_in_dim.38
  162.2 0.0 copy-start.3
  162.2 8.4 %fusion.18 = (bf16[512,512]{1,0:T(8,128)(2,1)}, f32[512,512]{1,0:T(8,128)}) fusion(f32[64,8,4,128]{3,2,1,0:T(4,128)S(1)} %bitcast.69, f32[512]{0:T(512)} %bitcast.73, bf16[1,4608,512]{2,1,0:T(8,128)(2,1)} %param.9, bf16[1,512,4608]{2,1,0:T(8,128)(2,1)} %all-gather.6.cloned.1.call-done), kind=kOutput, calls=%fused_computation.20 | convolution fusion | flops 2418278400 | bytes 12060672 | tf_op jit(solution)/shard_map/dot_general | solution.py:49
  170.6 1.3 collective-permute-start
  171.8 29.9 %collective-permute-done = bf16[512,512]{1,0:T(8,128)(2,1)S(1)} collective-permute-done((bf16[512,512]{1,0:T(8,128)(2,1)}, bf16[512,512]{1,0:T(8,128)(2,1)S(1)}, u32[]{:S(2)}, u32[]{:S(2)}) %collective-permute-start) | collective-permute-done | bytes 524320 | tf_op jit(solution)/shard_map/ppermute | solution.py:12
  201.8 5.2 broadcast_select_fusion
  207.0 0.0 reduce-scatter.5.cloned.1.call-update
  207.0 0.0 reduce-scatter.3.cloned.1.call-start
  207.0 10.2 %select_add_fusion = f32[512,4608]{1,0:T(8,128)} fusion(f32[512,2304]{1,0:T(8,128)} %get-tuple-element.25, bf16[512,512]{1,0:T(8,128)(2,1)} %get-tuple-element.22, bf16[1,512,4608]{2,1,0:T(8,128)(2,1)} %param.11, pred[]{:T(512)S(6)} %eq.22), kind=kOutput, calls=%fused_computation.1 | convolution fusion | flops 2420637696 | bytes 19398656 | tf_op jit(solution)/shard_map/dot_general | solution.py:54
  217.2 0.0 reduce-scatter.3.cloned.1.call-update
  217.3 0.0 copy-start.6
  217.3 0.0 all-gather.4.cloned.1.call-start
  217.3 203.6 %reduce-scatter.5.cloned.1.call-done = f32[8,2304]{1,0:T(8,128)} async-done(((f32[512,2304]{1,0:T(8,128)}), f32[8,2304]{1,0:T(8,128)}) %reduce-scatter.5.cloned.1.call-update) | async-done | bytes 73744 | tf_op jit(solution)/shard_map/reduce_scatter | solution.py:60
  420.9 1.3 collective-permute-start.1
  422.2 3.5 collective-permute-done.1
  425.7 224.2 %reduce-scatter.3.cloned.1.call-done = f32[8,4608]{1,0:T(8,128)} async-done(((f32[512,4608]{1,0:T(8,128)}), f32[8,4608]{1,0:T(8,128)}) %reduce-scatter.3.cloned.1.call-update) | async-done | bytes 147472 | tf_op jit(solution)/shard_map/reduce_scatter | solution.py:59
  649.9 1.6 fusion.23
  651.5 0.0 all-gather.4.cloned.1.call-update
  651.5 69.4 %all-gather.4.cloned.1.call-done = bf16[512,4608]{1,0:T(8,128)(2,1)} async-done(((bf16[8,4608]{1,0:T(8,128)(2,1)}), bf16[512,4608]{1,0:T(8,128)(2,1)}) %all-gather.4.cloned.1.call-update) | async-done | bytes 4718608 | tf_op jit(solution)/shard_map/all_gather | solution.py:65
  721.0 3.2 slice.10
  724.2 5.7 collective-permute-start.2
  729.9 6.1 all-to-all-start
  736.0 0.1 reshape.58
  736.1 12.1 %all-to-all-done = bf16[64,8,512]{2,1,0:T(8,128)(2,1)S(1)} async-done(((bf16[64,8,512]{2,1,0:T(8,128)(2,1)}), bf16[64,8,512]{2,1,0:T(8,128)(2,1)S(1)}, u32[]{:S(2)}, u32[]{:S(2)}) %all-to-all-start) | async-done | bytes 524320 | tf_op jit(solution)/shard_map/all_to_all | solution.py:77
  748.2 0.2 copy.15
  748.4 1.1 reshape.56
  749.5 2.3 gather_fusion
  751.7 0.0 collective-permute-done.2
  751.7 3.2 fusion.21
  755.0 0.0 slice-start.5
  755.0 2.1 collective-permute-start.3
  757.2 5.3 fusion.1
  762.5 2.9 convolution_convert_fusion.2
  765.4 0.0 collective-permute-done.3
  765.4 0.0 slice-done.4
  765.4 0.0 slice-start.3
  765.5 3.4 convert_reduce_fusion
  768.9 0.0 slice-done.2
  768.9 4.3 fusion
  773.2 6.6 copy.16
  (26 shorter events, 0.1 us)
Async XLA Ops:
  7.2 194.6 %copy-start = (bf16[512,2304]{1,0:T(8,128)(2,1)S(1)}, bf16[512,2304]{1,0:T(8,128)(2,1)}, u32[]{:S(2)}) copy-start(bf16[512,2304]{1,0:T(8,128)(2,1)} %param.12) | copy-start | bytes 7077892
  7.2 154.4 %all-gather.6.cloned.1.call-start = ((), (), s32[]{:S(2)}) async-start(), calls=%async_computation.6 | async-start | bytes 4792320 | tf_op jit(solution)/shard_map/all_gather | solution.py:44
  7.9 413.0 %reduce-scatter.5.cloned.1.call-start = ((), (), s32[]{:S(2)}) async-start(), calls=%async_computation.4 | async-start | bytes 4792320 | tf_op jit(solution)/shard_map/reduce_scatter | solution.py:60
  162.2 8.4 %copy-start.3 = (f32[512,4,128]{2,1,0:T(4,128)}, f32[512,4,128]{2,1,0:T(4,128)S(1)}, u32[]{:S(2)}) copy-start(f32[512,4,128]{2,1,0:T(4,128)S(1)} %broadcast_in_dim.38) | copy-start | bytes 3145732
  170.6 31.2 %collective-permute-start = (bf16[512,512]{1,0:T(8,128)(2,1)}, bf16[512,512]{1,0:T(8,128)(2,1)S(1)}, u32[]{:S(2)}, u32[]{:S(2)}) collective-permute-start(bf16[512,512]{1,0:T(8,128)(2,1)} %get-tuple-element.22), channel_id=1, source_target_pairs={{0,64},{1,65},{2,66},{3,67},{4,68},{5,69},{6,70},{7,71},{8,72},{9,... | collective-permute-start | bytes 1572872 | tf_op jit(solution)/shard_map/ppermute | solution.py:12
  201.8 5.2 copy-start.1
  207.0 442.9 %reduce-scatter.3.cloned.1.call-start = ((), (), s32[]{:S(2)}) async-start(), calls=%async_computation.3 | async-start | bytes 9584640 | tf_op jit(solution)/shard_map/reduce_scatter | solution.py:59
  217.2 432.7 %copy-start.5 = (bf16[1,8,4608]{2,1,0:T(8,128)(2,1)S(1)}, bf16[1,8,4608]{2,1,0:T(8,128)(2,1)}, u32[]{:S(2)}) copy-start(bf16[1,8,4608]{2,1,0:T(8,128)(2,1)} %param.8) | copy-start | bytes 221188
  217.3 518.7 %copy-start.6 = (s32[1,8,8]{2,1,0:T(8,128)S(1)}, s32[1,8,8]{2,1,0:T(8,128)}, u32[]{:S(2)}) copy-start(s32[1,8,8]{2,1,0:T(8,128)} %param.13) | copy-start | bytes 772
  217.3 503.7 %all-gather.4.cloned.1.call-start = ((), (), s32[]{:S(2)}) async-start(), calls=%async_computation.5 | async-start | bytes 4792320 | tf_op jit(solution)/shard_map/all_gather | solution.py:65
  420.9 4.8 collective-permute-start.1
  724.2 27.6 %collective-permute-start.2 = (bf16[512,2304]{1,0:T(8,128)(2,1)}, bf16[512,2304]{1,0:T(8,128)(2,1)}, u32[]{:S(2)}, u32[]{:S(2)}) collective-permute-start(bf16[512,2304]{1,0:T(8,128)(2,1)} %slice.10), channel_id=1, source_target_pairs={{64,0},{65,1},{66,2},{67,3},{68,4},{69,5},{70,6},{71,7},{72,8},{73... | collective-permute-start | bytes 7077896 | tf_op jit(solution)/shard_map/ppermute | solution.py:12
  729.9 18.3 %all-to-all-start = ((bf16[64,8,512]{2,1,0:T(8,128)(2,1)}), bf16[64,8,512]{2,1,0:T(8,128)(2,1)S(1)}, u32[]{:S(2)}, u32[]{:S(2)}) async-start(bf16[64,8,512]{2,1,0:T(8,128)(2,1)} %bitcast.6), calls=%async_computation.2 | async-start | bytes 1048576 | tf_op jit(solution)/shard_map/all_to_all | solution.py:77
  749.5 7.7 slice-start
  751.7 5.4 slice-start.1
  751.7 13.7 %slice-start.4 = ((s8[4718592]{0:T(1024)(128)(4,1)}), s8[4194304]{0:T(1024)(128)(4,1)S(1)}, s32[]{:S(2)}) async-start(s8[4718592]{0:T(1024)(128)(4,1)} %bitcast.66), calls=%async_computation.11 | async-start | bytes 8388608
  755.0 7.5 copy-start.2
  755.0 10.4 %slice-start.5 = ((s8[4718592]{0:T(1024)(128)(4,1)}), s8[524288]{0:T(1024)(128)(4,1)S(1)}, s32[]{:S(2)}) async-start(s8[4718592]{0:T(1024)(128)(4,1)} %bitcast.66), calls=%async_computation.12 | async-start | bytes 1048576
  755.0 10.4 %collective-permute-start.3 = (f32[512,512]{1,0:T(8,128)S(1)}, f32[512,512]{1,0:T(8,128)S(1)}, u32[]{:S(2)}, u32[]{:S(2)}) collective-permute-start(f32[512,512]{1,0:T(8,128)S(1)} %fusion.21), channel_id=1, source_target_pairs={{64,0},{65,1},{66,2},{67,3},{68,4},{69,5},{70,6},{71,7},{72,8},{73... | collective-permute-start | bytes 3145736 | tf_op jit(solution)/shard_map/ppermute | solution.py:12
  762.5 2.9 copy-start.4
  762.5 2.9 copy-start.7
  762.5 6.4 slice-start.2
  765.4 3.4 slice-start.3
Sparse Core Ops, SparseCore 0:
  10.9 71.6 all-gather.5
  207.1 213.7 reduce-scatter.4
  425.5 224.3 reduce-scatter.2
  653.6 67.3 all-gather.3
where the time goes:
time: 787 us; the launch traced here: 786 us
  waiting for transfers between devices  544 us (69%)
  blocking collectives  153 us (19%)
  matrix products  42.9 us (5%)
  starting transfers between devices  16.6 us (2%)
  local copies, waits for them, and re-layouts  14.1 us (2%)
  between operations  14 us (2%)
    reduce_scatter x1, waiting for transfers between devices, per_device(): lax.psum_scatter(main_term, 'feat', scatter_dimension=0, tiled=True)  224 us
    reduce_scatter x1, waiting for transfers between devices, per_device(): lax.psum_scatter(outgoing, 'feat', scatter_dimension=0, tiled=True)  204 us
    all_gather x1, blocking collectives, per_device(): lax.all_gather(block_table, 'feat', axis=0, tiled=True)  153 us
    all_gather x1, waiting for transfers between devices, per_device(): errors = lax.all_gather(errors_own, 'feat', axis=0, tiled=True)  69.4 us
    ppermute x4, waiting for transfers between devices, shifted(): return lax.ppermute(block, axis, route)  33.5 us
  transfers between devices with their start and end apart: 9, of which 6 were waited for; matrix products, arithmetic and copies ran while one was open for 3% of the time, Pallas kernels for 0%

commit v1 on v0

v1 whole, which is shorter than its diff:
```python
import jax
import jax.numpy as jnp
from jax import lax
from jax.sharding import PartitionSpec as P

BLK = 128
SIDE = 4
STEPS = {"y": (1, 0, 0), "x": (0, 1, 0), "z": (0, 0, 1)}


def route(axes, distance):
    pairs = []
    for core, axis in enumerate(axes):
        step = STEPS[axis]
        for y in range(SIDE):
            for x in range(SIDE):
                for z in range(SIDE):
                    there = [(c + distance * s) % SIDE for c, s in zip((y, x, z), step)]
                    base = core * SIDE**3
                    pairs.append(
                        (base + (y * SIDE + x) * SIDE + z, base + (there[0] * SIDE + there[1]) * SIDE + there[2])
                    )
    return pairs


def send(block, axes, distance):
    return lax.ppermute(block, ("layer", "feat"), route(axes, distance))


OUTER = ("z", "y")
MIDDLE = ("x", "x")
INNER = ("y", "z")


def line_gather(block, axes):
    return jnp.stack([block] + [send(block, axes, -r) for r in (1, 2, 3)])


def line_reduce(terms, axes):
    total = terms[0].astype(jnp.float32)
    for r in (1, 2, 3):
        total = total + send(terms[r].astype(jnp.bfloat16), axes, r).astype(jnp.float32)
    return total


def gather_tokens(rows, cut):
    inner = line_gather(rows, INNER)
    first, second = inner[..., :cut], inner[..., cut:]
    second = line_gather(second, OUTER)
    first = line_gather(first, MIDDLE)
    second = line_gather(second, MIDDLE)
    first = line_gather(first, OUTER)
    second = jnp.swapaxes(second, 0, 1)
    return first.reshape(-1, first.shape[-1]), second.reshape(-1, second.shape[-1])


def reduce_tokens(first, second):
    first = first.reshape(SIDE, SIDE, SIDE, -1, first.shape[-1])
    second = second.reshape(SIDE, SIDE, SIDE, -1, second.shape[-1])
    second = line_reduce([second[:, r] for r in range(SIDE)], MIDDLE)
    first = line_reduce([first[r] for r in range(SIDE)], OUTER)
    second = line_reduce([second[r] for r in range(SIDE)], OUTER)
    first = line_reduce([first[r] for r in range(SIDE)], MIDDLE)
    both = jnp.concatenate([first, second], axis=-1)
    return line_reduce([both[r] for r in range(SIDE)], INNER)


def other_order(rows):
    shape = (SIDE, SIDE, SIDE, -1, rows.shape[-1])
    return jnp.transpose(rows.reshape(shape), (2, 1, 0, 3, 4)).reshape(rows.shape)


def to_second(block):
    return lax.ppermute(block, "layer", [(0, 1)])


def to_first(block):
    return lax.ppermute(block, "layer", [(1, 0)])


def contract_rows(left, right):
    return lax.dot_general(left, right, (((0,), (0,)), ((), ())), preferred_element_type=jnp.float32)


def contract_cols(left, right):
    return lax.dot_general(left, right, (((1,), (1,)), ((), ())), preferred_element_type=jnp.float32)


def per_device(inputs, targets, w_enc, b_enc, w_self, w_cross, block_ids):
    first_layer = lax.axis_index("layer") == 0
    shard_index = lax.axis_index("feat")
    width = inputs.shape[2]
    half = width // 2
    latent_dev = w_enc.shape[2]
    blocks_dev = latent_dev // BLK
    slots = block_ids.shape[2]
    tokens_dev = inputs.shape[1]

    w_cross_first = to_second(w_cross)

    ids_bf = jnp.pad(block_ids[0].astype(jnp.bfloat16), ((0, 0), (0, BLK - slots)))
    cut = (2 * width // 3) // BLK * BLK
    x_first, x_second = gather_tokens(jnp.concatenate([inputs[0], ids_bf], axis=1), cut)
    ids = x_second[:, width - cut : width - cut + slots].astype(jnp.int32)
    x_second = x_second[:, : width - cut]
    tokens = x_first.shape[0]

    own_blocks = shard_index * blocks_dev + jnp.arange(blocks_dev, dtype=jnp.int32)
    hit = ids[:, :, None] == own_blocks[None, None, :]
    active = jnp.repeat(jnp.any(hit, axis=1), BLK, axis=1).astype(jnp.float32)
    x_all = jnp.concatenate([x_first, x_second], axis=1)
    pre = jnp.dot(x_all, w_enc[0], preferred_element_type=jnp.float32) + b_enc[0]
    codes = (active * jax.nn.softplus(pre)).astype(jnp.bfloat16)

    codes_turned = other_order(codes)
    earlier = to_second(codes_turned)
    source = jnp.where(first_layer, codes_turned, earlier)

    by_block = codes.reshape(tokens, 1, blocks_dev, BLK)
    slotted = jnp.sum(jnp.where(hit[..., None], by_block, 0).astype(jnp.float32), axis=2)
    slotted = slotted.reshape(tokens, slots * BLK)

    w_cross_all = jnp.concatenate([w_cross_first, w_cross], axis=1)
    self_part = jnp.dot(codes, w_self[0], preferred_element_type=jnp.float32)
    cross_part = jnp.dot(earlier, w_cross_all, preferred_element_type=jnp.float32)
    partial = self_part + jnp.where(first_layer, 0.0, cross_part)

    total_cols = width + slots * BLK
    rcut = (2 * total_cols // 3) // BLK * BLK
    summed = reduce_tokens(
        partial[:, :rcut], jnp.concatenate([partial[:, rcut:], slotted], axis=1)
    )
    recon_rows = summed[:, :width]
    picked = summed[:, width:].astype(jnp.bfloat16).reshape(tokens_dev, slots, BLK)

    err_own = (recon_rows - targets[0].astype(jnp.float32)).astype(jnp.bfloat16)
    err_first, err_second = gather_tokens(err_own, cut)
    err = jnp.concatenate([err_first, err_second], axis=1)

    cross_term = contract_cols(err, w_cross_all)
    back_term = other_order(to_first(cross_term))
    returned = to_first(err[:, :half])
    self_term = contract_cols(err, w_self[0])
    grad_self = contract_rows(codes, err).astype(jnp.bfloat16)
    cross_err = jnp.where(first_layer, returned, err[:, half:])
    grad_cross = contract_rows(source, cross_err).astype(jnp.bfloat16)
    code_grads = self_term + jnp.where(first_layer, back_term, 0.0)
    pre_grads = (code_grads * active * jax.nn.sigmoid(pre)).astype(jnp.bfloat16)
    grad_enc = contract_rows(x_all, pre_grads).astype(jnp.bfloat16)
    grad_benc = jnp.sum(pre_grads.astype(jnp.float32), axis=0)
    return (
        recon_rows[None],
        picked[None],
        grad_enc[None],
        grad_benc[None],
        grad_self[None],
        grad_cross,
    )


def solution(mesh):
    placed = (
        P("layer", "feat", None),
        P("layer", "feat", None),
        P("layer", None, "feat"),
        P("layer", "feat"),
        P("layer", "feat", None),
        P("feat", "layer"),
        P("layer", "feat", None),
    )
    return jax.shard_map(
        per_device,
        mesh=mesh,
        in_specs=placed,
        out_specs=(
            P("layer", "feat", None),
            P("layer", "feat", None, None),
            P("layer", None, "feat"),
            P("layer", "feat"),
            P("layer", "feat", None),
            P("feat", "layer"),
        ),
        check_vma=False,
    )
```

time: 787 us -> 230 us (0.29)
  waiting for transfers between devices: 544 us -> 67.2 us
  blocking collectives: 153 us -> 0 us
  starting transfers between devices: 16.6 us -> 93.4 us
  other arithmetic: 2.51 us -> 21.7 us
  between operations: 14 us -> 1.17 us
  matrix products: 42.9 us -> 33.2 us
    reduce_scatter x2 -> x0, waiting for transfers between devices: 428 us -> none  [the longest x1 224 us: per_device(): lax.psum_scatter(main_term, 'feat', scatter_dimension=0, tiled=True)]
    all_gather x1 -> x0, blocking collectives: 153 us -> none  [per_device(): lax.all_gather(block_table, 'feat', axis=0, tiled=True)]
    ppermute x4 -> x49, starting transfers between devices: 10.4 us -> 93.4 us  [the longest x45 64 us: send(): return lax.ppermute(block, ('layer', 'feat'), route(axes, distance))]
    all_gather x2 -> x0, waiting for transfers between devices: 69.4 us -> none  [the longest x1 69.4 us: per_device(): errors = lax.all_gather(errors_own, 'feat', axis=0, tiled=True)]
    ppermute x4 -> x49, waiting for transfers between devices: 33.5 us -> 67.2 us  [the longest x45 67.2 us: send(): return lax.ppermute(block, ('layer', 'feat'), route(axes, distance))]
    reduce_sum x0 -> x1, other arithmetic: none -> 12.9 us  [per_device(): jnp.sum(jnp.where(hit[..., None], by_block, 0).astype(jnp.float32), axis=2)]
    all_to_all x1 -> x0, waiting for transfers between devices: 12.1 us -> none  [per_device(): lax.all_to_all(latent_codes, 'feat', split_axis=0, concat_axis=1, tiled=T...]
    dot_general x3, matrix products: 23.7 us -> 15.4 us  [the longest x1 6.6 us: per_device(): jnp.dot(x_all, w_enc[0], preferred_element_type=jnp.float32) + b_enc[0]]
  transfers between devices with their start and end apart: 9 -> 49, of which waited for: 6 -> 26; matrix products, arithmetic and copies ran while one was open for 3% -> 23% of each run, Pallas kernels for 0% -> 0%
where the time goes in v1:
time: 230 us
  starting transfers between devices  93.4 us (41%)
  waiting for transfers between devices  67.2 us (29%)
  matrix products  33.2 us (14%)
  other arithmetic  21.7 us (9%)
  local copies, waits for them, and re-layouts  13.3 us (6%)
    ppermute x45, waiting for transfers between devices, send(): return lax.ppermute(block, ('layer', 'feat'), route(axes, distance))  67.2 us
    ppermute x45, starting transfers between devices, send(): return lax.ppermute(block, ('layer', 'feat'), route(axes, distance))  64 us
    ppermute x2, starting transfers between devices, to_first(): return lax.ppermute(block, 'layer', [(1, 0)])  26.6 us
    reduce_sum x1, other arithmetic, per_device(): jnp.sum(jnp.where(hit[..., None], by_block, 0).astype(jnp.float32), axis=2)  12.9 us
    dot_general x3, matrix products, contract_rows(): lax.dot_general(left, right, (((0,), (0,)), ((), ())), preferred_element_...  11.7 us
    dot_general x1, matrix products, per_device(): jnp.dot(x_all, w_enc[0], preferred_element_type=jnp.float32) + b_enc[0]  6.6 us
    dot_general x2, matrix products, contract_cols(): lax.dot_general(left, right, (((1,), (1,)), ((), ())), preferred_element_...  6.07 us
    another operation x14, other arithmetic, line_gather(): return jnp.stack([block] + [send(block, axes, -r) for r in (1, 2, 3)])  5.96 us
  transfers between devices with their start and end apart: 49, of which 26 were waited for; matrix products, arithmetic and copies ran while one was open for 23% of the time, Pallas kernels for 0%

profile of v1, /device:TPU:1, one launch (start us, length us, event | category | flops | bytes accessed | tf_op | source)
XLA Modules:
  0.0 229.9 jit_solution(7054633187222301745)
XLA Ops:
  2.2 2.5 %collective-permute-start.2 = (bf16[8,4736]{1,0:T(8,128)(2,1)S(1)}, bf16[8,4736]{1,0:T(8,128)(2,1)S(1)}, u32[]{:S(2)}, u32[]{:S(2)}) collective-permute-start(bf16[8,4736]{1,0:T(8,128)(2,1)S(1)} %get-tuple-element.58), channel_id=1, source_target_pairs={{0,16},{1,17},{2,18},{3,19},{4,20},{5,21},{6,22},{7,23},{8,24},{9,... | collective-permute-start | bytes 227336 | tf_op jit(solution)/shard_map/ppermute | solution.py:27
  4.8 3.3 %collective-permute-start.1 = (bf16[8,4736]{1,0:T(8,128)(2,1)S(1)}, bf16[8,4736]{1,0:T(8,128)(2,1)S(1)}, u32[]{:S(2)}, u32[]{:S(2)}) collective-permute-start(bf16[8,4736]{1,0:T(8,128)(2,1)S(1)} %get-tuple-element.58), channel_id=1, source_target_pairs={{0,32},{1,33},{2,34},{3,35},{4,36},{5,37},{6,38},{7,39},{8,40},{9,... | collective-permute-start | bytes 227336 | tf_op jit(solution)/shard_map/ppermute | solution.py:27
  8.9 2.0 collective-permute-done.1
  12.7 2.9 %collective-permute-start.4 = (bf16[4,8,1664]{2,1,0:T(8,128)(2,1)S(1)}, bf16[4,8,1664]{2,1,0:T(8,128)(2,1)S(1)}, u32[]{:S(2)}, u32[]{:S(2)}) collective-permute-start(bf16[4,8,1664]{2,1,0:T(8,128)(2,1)S(1)} %pad_maximum_fusion.31), channel_id=1, source_target_pairs={{0,2},{1,3},{2,0},{3,1},{4,6},{5,7},{6,4},{7,5},{8,10},{9,11},{10,... | collective-permute-start | bytes 319496 | tf_op jit(solution)/shard_map/ppermute | solution.py:27
  17.7 2.5 %collective-permute-start.10 = (bf16[4,8,3072]{2,1,0:T(8,128)(2,1)S(1)}, bf16[4,8,3072]{2,1,0:T(8,128)(2,1)S(1)}, u32[]{:S(2)}, u32[]{:S(2)}) collective-permute-start(bf16[4,8,3072]{2,1,0:T(8,128)(2,1)S(1)} %pad_maximum_fusion.28), channel_id=1, source_target_pairs={{0,8},{1,9},{2,10},{3,11},{4,12},{5,13},{6,14},{7,15},{8,0},{9,1},... | collective-permute-start | bytes 589832 | tf_op jit(solution)/shard_map/ppermute | solution.py:27
  24.3 1.8 collective-permute-done.10
  28.6 10.1 %collective-permute-done.8 = bf16[4,4,8,1664]{3,2,1,0:T(8,128)(2,1)S(1)} collective-permute-done((bf16[4,4,8,1664]{3,2,1,0:T(8,128)(2,1)S(1)}, bf16[4,4,8,1664]{3,2,1,0:T(8,128)(2,1)S(1)}, u32[]{:S(2)}, u32[]{:S(2)}) %collective-permute-start.8) | collective-permute-done | bytes 426016 | tf_op jit(solution)/shard_map/ppermute | solution.py:27
  39.5 5.3 %collective-permute-done.7 = bf16[4,4,8,1664]{3,2,1,0:T(8,128)(2,1)} collective-permute-done((bf16[4,4,8,1664]{3,2,1,0:T(8,128)(2,1)S(1)}, bf16[4,4,8,1664]{3,2,1,0:T(8,128)(2,1)}, u32[]{:S(2)}, u32[]{:S(2)}) %collective-permute-start.7) | collective-permute-done | bytes 426016 | tf_op jit(solution)/shard_map/ppermute | solution.py:27
  46.0 1.5 pad_maximum_fusion.7
  50.8 1.5 pad_maximum_fusion.3
  52.4 1.6 broadcast_in_dim.46
  54.0 6.6 %fusion.29 = (bf16[512,512]{1,0:T(8,128)(2,1)S(1)}, f32[512,512]{1,0:T(8,128)}) fusion(pred[64,8,4,128]{3,2,1,0:T(4,128)(4,1)S(1)} %bitcast.254, f32[512]{0:T(512)S(1)} %bitcast.269, bf16[1,4608,512]{2,1,0:T(8,128)(2,1)} %param.9, bf16[512,1536]{1,0:T(8,128)(2,1)S(1)} %copy-done.3, bf16[512,3072]{1,0:T(8,128)(2,1)S(1)} %bitcast.215), kind=kOutput, calls=%fused_computation.36 | convolution fusion | flops 2427715584 | bytes 11274240 | tf_op jit(solution)/shard_map/dot_general | solution.py:112
  63.0 12.9 %convert_reduce_fusion = f32[512,8,128]{2,1,0:T(8,128)} fusion(pred[512,8,4]{1,2,0:T(4,128)(4,1)S(1)} %copy.49, bf16[512,4,128]{2,1,0:T(4,128)(2,1)S(1)} %broadcast_in_dim.49), kind=kLoop, calls=%fused_computation.1 | loop fusion | flops 5767168 | bytes 2637824 | tf_op jit(solution)/shard_map/reduce_sum | solution.py:120
  75.9 1.7 concatenate.27
  77.7 4.5 %fusion.4 = f32[512,4608]{1,0:T(8,128)S(1)} fusion(bf16[512,512]{1,0:T(8,128)(2,1)S(1)} %get-tuple-element.59, bf16[1,512,4608]{2,1,0:T(8,128)(2,1)} %param.11), kind=kOutput, calls=%fused_computation.12 | convolution fusion | flops 2415919104 | bytes 14680064 | tf_op jit(solution)/shard_map/dot_general | solution.py:124
  82.2 1.8 constant_dynamic-update-slice_fusion.1
  84.0 1.8 constant_dynamic-update-slice_fusion
  85.9 4.3 %fusion.69 = (bf16[512,4608]{1,0:T(8,128)(2,1)}, f32[512,4608]{1,0:T(8,128)S(1)}) fusion(f32[512,4608]{1,0:T(8,128)S(1)} %fusion.4, bf16[512,512]{1,0:T(8,128)(2,1)S(1)} %collective-permute-done.15, bf16[512,4608]{1,0:T(8,128)(2,1)S(1)} %constant_dynamic-update-slice_fusion, pred[]{:T(512)S(6)} %eq.23), kind=kOutput, calls=%fused_computation.114 | convolution fusion | flops 2422996992 | bytes 28835840 | tf_op jit(solution)/shard_map/dot_general | solution.py:125
  94.8 1.5 collective-permute-start.18
  96.3 2.2 collective-permute-done.25
  98.9 2.0 collective-permute-done.24
  100.9 5.2 %collective-permute-done.23 = bf16[4,4,8,1920]{3,2,1,0:T(8,128)(2,1)S(1)} collective-permute-done((bf16[4,4,8,1920]{3,2,1,0:T(8,128)(2,1)S(1)}, bf16[4,4,8,1920]{3,2,1,0:T(8,128)(2,1)S(1)}, u32[]{:S(2)}, u32[]{:S(2)}) %collective-permute-start.23) | collective-permute-done | bytes 491552 | tf_op jit(solution)/shard_map/ppermute | solution.py:27
  106.4 1.5 collective-permute-start.28
  109.0 8.6 %collective-permute-start.26 = (bf16[4,8,1920]{2,1,0:T(8,128)(2,1)S(1)}, bf16[4,8,1920]{2,1,0:T(8,128)(2,1)S(1)}, u32[]{:S(2)}, u32[]{:S(2)}) collective-permute-start(bf16[4,8,1920]{2,1,0:T(8,128)(2,1)S(1)} %get-tuple-element.43), channel_id=1, source_target_pairs={{0,1},{1,2},{2,3},{3,0},{4,5},{5,6},{6,7},{7,4},{8,9},{9,10},{10,1... | collective-permute-start | bytes 368648 | tf_op jit(solution)/shard_map/ppermute | solution.py:27
  117.6 1.8 collective-permute-done.17
  119.9 2.1 collective-permute-start.22
  123.4 4.2 %collective-permute-done.22 = bf16[4,8,3712]{2,1,0:T(8,128)(2,1)S(1)} collective-permute-done((bf16[4,8,3712]{2,1,0:T(8,128)(2,1)S(1)}, bf16[4,8,3712]{2,1,0:T(8,128)(2,1)S(1)}, u32[]{:S(2)}, u32[]{:S(2)}) %collective-permute-start.22) | collective-permute-done | bytes 237600 | tf_op jit(solution)/shard_map/ppermute | solution.py:27
  128.6 2.7 %collective-permute-done.20 = bf16[4,8,3712]{2,1,0:T(8,128)(2,1)S(1)} collective-permute-done((bf16[4,8,3712]{2,1,0:T(8,128)(2,1)S(1)}, bf16[4,8,3712]{2,1,0:T(8,128)(2,1)S(1)}, u32[]{:S(2)}, u32[]{:S(2)}) %collective-permute-start.20) | collective-permute-done | bytes 237600 | tf_op jit(solution)/shard_map/ppermute | solution.py:27
  131.5 5.7 %collective-permute-start.31 = (bf16[8,5632]{1,0:T(8,128)(2,1)S(1)}, bf16[8,5632]{1,0:T(8,128)(2,1)S(1)}, u32[]{:S(2)}, u32[]{:S(2)}) collective-permute-start(bf16[8,5632]{1,0:T(8,128)(2,1)S(1)} %get-tuple-element.51), channel_id=1, source_target_pairs={{0,48},{1,49},{2,50},{3,51},{4,52},{5,53},{6,54},{7,55},{8,56},{9,... | collective-permute-start | bytes 270344 | tf_op jit(solution)/shard_map/ppermute | solution.py:27
  137.9 1.8 collective-permute-done.31
  139.6 2.5 %collective-permute-done.30 = bf16[8,5632]{1,0:T(8,128)(2,1)S(1)} collective-permute-done((bf16[8,5632]{1,0:T(8,128)(2,1)S(1)}, bf16[8,5632]{1,0:T(8,128)(2,1)S(1)}, u32[]{:S(2)}, u32[]{:S(2)}) %collective-permute-start.30) | collective-permute-done | bytes 90144 | tf_op jit(solution)/shard_map/ppermute | solution.py:27
  143.5 1.8 collective-permute-start.33
  146.5 2.2 collective-permute-done.34
  149.6 2.0 collective-permute-start.42
  154.5 1.8 collective-permute-done.43
  157.9 2.9 %collective-permute-done.37 = bf16[4,8,3072]{2,1,0:T(8,128)(2,1)S(1)} collective-permute-done((bf16[4,8,3072]{2,1,0:T(8,128)(2,1)S(1)}, bf16[4,8,3072]{2,1,0:T(8,128)(2,1)S(1)}, u32[]{:S(2)}, u32[]{:S(2)}) %collective-permute-start.37) | collective-permute-done | bytes 196640 | tf_op jit(solution)/shard_map/ppermute | solution.py:27
  162.2 1.6 collective-permute-start.39
  163.8 2.0 collective-permute-start.38
  167.2 1.5 collective-permute-start.44
  168.7 5.7 %collective-permute-done.45 = bf16[4,4,8,1536]{3,2,1,0:T(8,128)(2,1)S(1)} collective-permute-done((bf16[4,4,8,1536]{3,2,1,0:T(8,128)(2,1)S(1)}, bf16[4,4,8,1536]{3,2,1,0:T(8,128)(2,1)S(1)}, u32[]{:S(2)}, u32[]{:S(2)}) %collective-permute-start.45) | collective-permute-done | bytes 393248 | tf_op jit(solution)/shard_map/ppermute | solution.py:27
  174.5 6.9 %collective-permute-done.44 = bf16[4,4,8,1536]{3,2,1,0:T(8,128)(2,1)S(1)} collective-permute-done((bf16[4,4,8,1536]{3,2,1,0:T(8,128)(2,1)S(1)}, bf16[4,4,8,1536]{3,2,1,0:T(8,128)(2,1)S(1)}, u32[]{:S(2)}, u32[]{:S(2)}) %collective-permute-start.44) | collective-permute-done | bytes 393248 | tf_op jit(solution)/shard_map/ppermute | solution.py:27
  183.5 2.6 %fusion.12 = f32[512,512]{1,0:T(8,128)S(1)} fusion(bf16[512,4608]{1,0:T(8,128)(2,1)S(1)} %bitcast.203, bf16[512,1536]{1,0:T(8,128)(2,1)S(1)} %bitcast.207, bf16[512,3072]{1,0:T(8,128)(2,1)S(1)} %bitcast.193), kind=kOutput, calls=%fused_computation.29 | convolution fusion | flops 2425356288 | bytes 10485760 | tf_op jit(solution)/shard_map/dot_general | solution.py:86
  186.1 24.6 %collective-permute-start.47 = (f32[512,512]{1,0:T(8,128)S(1)}, f32[512,512]{1,0:T(8,128)S(1)}, u32[]{:S(2)}, u32[]{:S(2)}) collective-permute-start(f32[512,512]{1,0:T(8,128)S(1)} %fusion.12), channel_id=1, source_target_pairs={{64,0},{65,1},{66,2},{67,3},{68,4},{69,5},{70,6},{71,7},{72,8},{73... | collective-permute-start | bytes 3145736 | tf_op jit(solution)/shard_map/ppermute | solution.py:78
  210.9 2.0 collective-permute-start.48
  213.6 4.4 %fusion.1 = bf16[1,512,4608]{2,1,0:T(8,128)(2,1)} fusion(bf16[512,512]{1,0:T(8,128)(2,1)S(1)} %get-tuple-element.59, bf16[512,1536]{1,0:T(8,128)(2,1)S(1)} %bitcast.208, bf16[512,3072]{1,0:T(8,128)(2,1)S(1)} %bitcast.195), kind=kOutput, calls=%fused_computation.5 | convolution fusion | flops 2427715584 | bytes 9961472 | tf_op jit(solution)/shard_map/dot_general | solution.py:82
  219.2 3.4 %convert_reduce_fusion.1 = (f32[512]{0:T(512)}, bf16[512,512]{1,0:T(8,128)(2,1)S(1)}) fusion(f32[512,512]{1,0:T(8,128)S(1)} %copy-done.8, f32[512,512]{1,0:T(8,128)S(1)} %bitcast.232, bf16[1,512,4608]{2,1,0:T(8,128)(2,1)S(1)} %bitcast.212, bf16[512,1536]{1,0:T(8,128)(2,1)S(1)} %bitcast.209, bf16[512,3072]{1,0:T(8,128)(2,1)S(1)} %bitcast.196, ...), kind=kOutput, calls=%fused_computation.37 | convolution fusion | flops 2427715072 | bytes 12322816 | tf_op jit(solution)/shard_map/dot_general | solution.py:86
  222.7 4.3 %fusion = bf16[1,4608,512]{2,1,0:T(8,128)(2,1)} fusion(bf16[512,512]{1,0:T(8,128)(2,1)S(1)} %get-tuple-element.64, bf16[512,1536]{1,0:T(8,128)(2,1)S(1)} %copy-done.4, bf16[512,3072]{1,0:T(8,128)(2,1)S(1)} %bitcast.216), kind=kOutput, calls=%fused_computation.4 | convolution fusion | flops 2427715584 | bytes 9961472 | tf_op jit(solution)/shard_map/dot_general | solution.py:82
  227.0 2.9 %convolution_convert_fusion.2 = bf16[512,2304]{1,0:T(8,128)(2,1)} fusion(bf16[512,2304]{1,0:T(8,128)(2,1)S(1)} %collective-permute-done.48, bf16[512,1536]{1,0:T(8,128)(2,1)S(1)} %bitcast.210, bf16[512,3072]{1,0:T(8,128)(2,1)S(1)} %bitcast.197, pred[]{:T(512)S(6)} %eq.23, bf16[512,512]{1,0:T(8,128)(2,1)} %bitcast.34, ...), kind=kOutput, calls=%fused_computation.17 | convolution fusion | flops 1215299584 | bytes 10485761 | tf_op jit(solution)/shard_map/dot_general | solution.py:82
  (144 shorter events, 45.5 us)
Async XLA Ops:
  2.2 6.7 %collective-permute-start.2 = (bf16[8,4736]{1,0:T(8,128)(2,1)S(1)}, bf16[8,4736]{1,0:T(8,128)(2,1)S(1)}, u32[]{:S(2)}, u32[]{:S(2)}) collective-permute-start(bf16[8,4736]{1,0:T(8,128)(2,1)S(1)} %get-tuple-element.58), channel_id=1, source_target_pairs={{0,16},{1,17},{2,18},{3,19},{4,20},{5,21},{6,22},{7,23},{8,24},{9,... | collective-permute-start | bytes 227336 | tf_op jit(solution)/shard_map/ppermute | solution.py:27
  4.8 6.2 %collective-permute-start.1 = (bf16[8,4736]{1,0:T(8,128)(2,1)S(1)}, bf16[8,4736]{1,0:T(8,128)(2,1)S(1)}, u32[]{:S(2)}, u32[]{:S(2)}) collective-permute-start(bf16[8,4736]{1,0:T(8,128)(2,1)S(1)} %get-tuple-element.58), channel_id=1, source_target_pairs={{0,32},{1,33},{2,34},{3,35},{4,36},{5,37},{6,38},{7,39},{8,40},{9,... | collective-permute-start | bytes 227336 | tf_op jit(solution)/shard_map/ppermute | solution.py:27
  11.6 8.5 %collective-permute-start.5 = (bf16[4,8,1664]{2,1,0:T(8,128)(2,1)S(1)}, bf16[4,8,1664]{2,1,0:T(8,128)(2,1)S(1)}, u32[]{:S(2)}, u32[]{:S(2)}) collective-permute-start(bf16[4,8,1664]{2,1,0:T(8,128)(2,1)S(1)} %pad_maximum_fusion.31), channel_id=1, source_target_pairs={{0,1},{1,2},{2,3},{3,0},{4,5},{5,6},{6,7},{7,4},{8,9},{9,10},{10,1... | collective-permute-start | bytes 319496 | tf_op jit(solution)/shard_map/ppermute | solution.py:27
  12.7 8.6 %collective-permute-start.4 = (bf16[4,8,1664]{2,1,0:T(8,128)(2,1)S(1)}, bf16[4,8,1664]{2,1,0:T(8,128)(2,1)S(1)}, u32[]{:S(2)}, u32[]{:S(2)}) collective-permute-start(bf16[4,8,1664]{2,1,0:T(8,128)(2,1)S(1)} %pad_maximum_fusion.31), channel_id=1, source_target_pairs={{0,2},{1,3},{2,0},{3,1},{4,6},{5,7},{6,4},{7,5},{8,10},{9,11},{10,... | collective-permute-start | bytes 319496 | tf_op jit(solution)/shard_map/ppermute | solution.py:27
  15.6 5.7 %collective-permute-start.3 = (bf16[4,8,1664]{2,1,0:T(8,128)(2,1)S(1)}, bf16[4,8,1664]{2,1,0:T(8,128)(2,1)S(1)}, u32[]{:S(2)}, u32[]{:S(2)}) collective-permute-start(bf16[4,8,1664]{2,1,0:T(8,128)(2,1)S(1)} %pad_maximum_fusion.31), channel_id=1, source_target_pairs={{0,3},{1,0},{2,1},{3,2},{4,7},{5,4},{6,5},{7,6},{8,11},{9,8},{10,9... | collective-permute-start | bytes 319496 | tf_op jit(solution)/shard_map/ppermute | solution.py:27
  16.4 6.7 %collective-permute-start.11 = (bf16[4,8,3072]{2,1,0:T(8,128)(2,1)S(1)}, bf16[4,8,3072]{2,1,0:T(8,128)(2,1)S(1)}, u32[]{:S(2)}, u32[]{:S(2)}) collective-permute-start(bf16[4,8,3072]{2,1,0:T(8,128)(2,1)S(1)} %pad_maximum_fusion.28), channel_id=1, source_target_pairs={{0,4},{1,5},{2,6},{3,7},{4,8},{5,9},{6,10},{7,11},{8,12},{9,13},{1... | collective-permute-start | bytes 589832 | tf_op jit(solution)/shard_map/ppermute | solution.py:27
  17.7 8.4 %collective-permute-start.10 = (bf16[4,8,3072]{2,1,0:T(8,128)(2,1)S(1)}, bf16[4,8,3072]{2,1,0:T(8,128)(2,1)S(1)}, u32[]{:S(2)}, u32[]{:S(2)}) collective-permute-start(bf16[4,8,3072]{2,1,0:T(8,128)(2,1)S(1)} %pad_maximum_fusion.28), channel_id=1, source_target_pairs={{0,8},{1,9},{2,10},{3,11},{4,12},{5,13},{6,14},{7,15},{8,0},{9,1},... | collective-permute-start | bytes 589832 | tf_op jit(solution)/shard_map/ppermute | solution.py:27
  20.1 6.0 %collective-permute-start.9 = (bf16[4,8,3072]{2,1,0:T(8,128)(2,1)S(1)}, bf16[4,8,3072]{2,1,0:T(8,128)(2,1)S(1)}, u32[]{:S(2)}, u32[]{:S(2)}) collective-permute-start(bf16[4,8,3072]{2,1,0:T(8,128)(2,1)S(1)} %pad_maximum_fusion.28), channel_id=1, source_target_pairs={{0,12},{1,13},{2,14},{3,15},{4,0},{5,1},{6,2},{7,3},{8,4},{9,5},{1... | collective-permute-start | bytes 589832 | tf_op jit(solution)/shard_map/ppermute | solution.py:27
  21.4 17.3 %collective-permute-start.8 = (bf16[4,4,8,1664]{3,2,1,0:T(8,128)(2,1)S(1)}, bf16[4,4,8,1664]{3,2,1,0:T(8,128)(2,1)S(1)}, u32[]{:S(2)}, u32[]{:S(2)}) collective-permute-start(bf16[4,4,8,1664]{3,2,1,0:T(8,128)(2,1)S(1)} %get-tuple-element.47), channel_id=1, source_target_pairs={{0,4},{1,5},{2,6},{3,7},{4,8},{5,9},{6,10},{7,11},{8,12},{9,13},{1... | collective-permute-start | bytes 1277960 | tf_op jit(solution)/shard_map/ppermute | solution.py:27
  21.8 23.0 %collective-permute-start.7 = (bf16[4,4,8,1664]{3,2,1,0:T(8,128)(2,1)S(1)}, bf16[4,4,8,1664]{3,2,1,0:T(8,128)(2,1)}, u32[]{:S(2)}, u32[]{:S(2)}) collective-permute-start(bf16[4,4,8,1664]{3,2,1,0:T(8,128)(2,1)S(1)} %get-tuple-element.47), channel_id=1, source_target_pairs={{0,8},{1,9},{2,10},{3,11},{4,12},{5,13},{6,14},{7,15},{8,0},{9,1},... | collective-permute-start | bytes 1277960 | tf_op jit(solution)/shard_map/ppermute | solution.py:27
  23.1 23.0 %collective-permute-start.6 = (bf16[4,4,8,1664]{3,2,1,0:T(8,128)(2,1)S(1)}, bf16[4,4,8,1664]{3,2,1,0:T(8,128)(2,1)}, u32[]{:S(2)}, u32[]{:S(2)}) collective-permute-start(bf16[4,4,8,1664]{3,2,1,0:T(8,128)(2,1)S(1)} %get-tuple-element.47), channel_id=1, source_target_pairs={{0,12},{1,13},{2,14},{3,15},{4,0},{5,1},{6,2},{7,3},{8,4},{9,5},{1... | collective-permute-start | bytes 1277960 | tf_op jit(solution)/shard_map/ppermute | solution.py:27
  27.1 22.6 %collective-permute-start.14 = (bf16[4,4,8,3072]{3,2,1,0:T(8,128)(2,1)}, bf16[4,4,8,3072]{3,2,1,0:T(8,128)(2,1)S(1)}, u32[]{:S(2)}, u32[]{:S(2)}) collective-permute-start(bf16[4,4,8,3072]{3,2,1,0:T(8,128)(2,1)} %get-tuple-element.42), channel_id=1, source_target_pairs={{0,1},{1,2},{2,3},{3,0},{4,5},{5,6},{6,7},{7,4},{8,9},{9,10},{10,1... | collective-permute-start | bytes 2359304 | tf_op jit(solution)/shard_map/ppermute | solution.py:27
  28.3 21.4 %collective-permute-start.13 = (bf16[4,4,8,3072]{3,2,1,0:T(8,128)(2,1)}, bf16[4,4,8,3072]{3,2,1,0:T(8,128)(2,1)S(1)}, u32[]{:S(2)}, u32[]{:S(2)}) collective-permute-start(bf16[4,4,8,3072]{3,2,1,0:T(8,128)(2,1)} %get-tuple-element.42), channel_id=1, source_target_pairs={{0,2},{1,3},{2,0},{3,1},{4,6},{5,7},{6,4},{7,5},{8,10},{9,11},{10,... | collective-permute-start | bytes 2359304 | tf_op jit(solution)/shard_map/ppermute | solution.py:27
  39.5 11.3 %collective-permute-start.12 = (bf16[4,4,8,3072]{3,2,1,0:T(8,128)(2,1)}, bf16[4,4,8,3072]{3,2,1,0:T(8,128)(2,1)}, u32[]{:S(2)}, u32[]{:S(2)}) collective-permute-start(bf16[4,4,8,3072]{3,2,1,0:T(8,128)(2,1)} %get-tuple-element.42), channel_id=1, source_target_pairs={{0,3},{1,0},{2,1},{3,2},{4,7},{5,4},{6,5},{7,6},{8,11},{9,8},{10,9... | collective-permute-start | bytes 2359304 | tf_op jit(solution)/shard_map/ppermute | solution.py:27
  44.7 37.4 %collective-permute-start.16 = (bf16[512,2304]{1,0:T(8,128)(2,1)}, bf16[512,2304]{1,0:T(8,128)(2,1)}, u32[]{:S(2)}, u32[]{:S(2)}) collective-permute-start(bf16[512,2304]{1,0:T(8,128)(2,1)} %param.12), channel_id=1, source_target_pairs={{0,64},{1,65},{2,66},{3,67},{4,68},{5,69},{6,70},{7,71},{8,72},{9,... | collective-permute-start | bytes 7077896 | tf_op jit(solution)/shard_map/ppermute | solution.py:74
  61.6 24.3 %collective-permute-start.15 = (bf16[512,512]{1,0:T(8,128)(2,1)}, bf16[512,512]{1,0:T(8,128)(2,1)S(1)}, u32[]{:S(2)}, u32[]{:S(2)}) collective-permute-start(bf16[512,512]{1,0:T(8,128)(2,1)} %bitcast.34), channel_id=1, source_target_pairs={{0,64},{1,65},{2,66},{3,67},{4,68},{5,69},{6,70},{7,71},{8,72},{9,... | collective-permute-start | bytes 1572872 | tf_op jit(solution)/shard_map/ppermute | solution.py:74
  90.8 7.7 %collective-permute-start.25 = (bf16[4,4,8,1920]{3,2,1,0:T(8,128)(2,1)S(1)}, bf16[4,4,8,1920]{3,2,1,0:T(8,128)(2,1)S(1)}, u32[]{:S(2)}, u32[]{:S(2)}) collective-permute-start(bf16[4,4,8,1920]{3,2,1,0:T(8,128)(2,1)S(1)} %get-tuple-element.34), channel_id=1, source_target_pairs={{0,12},{1,13},{2,14},{3,15},{4,0},{5,1},{6,2},{7,3},{8,4},{9,5},{1... | collective-permute-start | bytes 1474568 | tf_op jit(solution)/shard_map/ppermute | solution.py:27
  91.7 9.3 %collective-permute-start.24 = (bf16[4,4,8,1920]{3,2,1,0:T(8,128)(2,1)S(1)}, bf16[4,4,8,1920]{3,2,1,0:T(8,128)(2,1)S(1)}, u32[]{:S(2)}, u32[]{:S(2)}) collective-permute-start(bf16[4,4,8,1920]{3,2,1,0:T(8,128)(2,1)S(1)} %get-tuple-element.35), channel_id=1, source_target_pairs={{0,8},{1,9},{2,10},{3,11},{4,12},{5,13},{6,14},{7,15},{8,0},{9,1},... | collective-permute-start | bytes 1474568 | tf_op jit(solution)/shard_map/ppermute | solution.py:27
  93.1 13.0 %collective-permute-start.23 = (bf16[4,4,8,1920]{3,2,1,0:T(8,128)(2,1)S(1)}, bf16[4,4,8,1920]{3,2,1,0:T(8,128)(2,1)S(1)}, u32[]{:S(2)}, u32[]{:S(2)}) collective-permute-start(bf16[4,4,8,1920]{3,2,1,0:T(8,128)(2,1)S(1)} %get-tuple-element.33), channel_id=1, source_target_pairs={{0,4},{1,5},{2,6},{3,7},{4,8},{5,9},{6,10},{7,11},{8,12},{9,13},{1... | collective-permute-start | bytes 1474568 | tf_op jit(solution)/shard_map/ppermute | solution.py:27
  93.5 15.5 %collective-permute-start.19 = (bf16[4,4,8,3712]{3,2,1,0:T(8,128)(2,1)S(1)}, bf16[4,4,8,3712]{3,2,1,0:T(8,128)(2,1)S(1)}, u32[]{:S(2)}, u32[]{:S(2)}) collective-permute-start(bf16[4,4,8,3712]{3,2,1,0:T(8,128)(2,1)S(1)} %bitcast.235), channel_id=1, source_target_pairs={{0,3},{1,0},{2,1},{3,2},{4,7},{5,4},{6,5},{7,6},{8,11},{9,8},{10,9... | collective-permute-start | bytes 2850824 | tf_op jit(solution)/shard_map/ppermute | solution.py:27
  94.8 22.8 %collective-permute-start.18 = (bf16[4,4,8,3712]{3,2,1,0:T(8,128)(2,1)S(1)}, bf16[4,4,8,3712]{3,2,1,0:T(8,128)(2,1)S(1)}, u32[]{:S(2)}, u32[]{:S(2)}) collective-permute-start(bf16[4,4,8,3712]{3,2,1,0:T(8,128)(2,1)S(1)} %bitcast.234), channel_id=1, source_target_pairs={{0,2},{1,3},{2,0},{3,1},{4,6},{5,7},{6,4},{7,5},{8,10},{9,11},{10,... | collective-permute-start | bytes 2850824 | tf_op jit(solution)/shard_map/ppermute | solution.py:27
  98.5 20.9 %collective-permute-start.17 = (bf16[4,4,8,3712]{3,2,1,0:T(8,128)(2,1)S(1)}, bf16[4,4,8,3712]{3,2,1,0:T(8,128)(2,1)S(1)}, u32[]{:S(2)}, u32[]{:S(2)}) collective-permute-start(bf16[4,4,8,3712]{3,2,1,0:T(8,128)(2,1)S(1)} %bitcast.233), channel_id=1, source_target_pairs={{0,1},{1,2},{2,3},{3,0},{4,5},{5,6},{6,7},{7,4},{8,9},{9,10},{10,1... | collective-permute-start | bytes 2850824 | tf_op jit(solution)/shard_map/ppermute | solution.py:27
  106.4 16.7 %collective-permute-start.28 = (bf16[4,8,1920]{2,1,0:T(8,128)(2,1)S(1)}, bf16[4,8,1920]{2,1,0:T(8,128)(2,1)S(1)}, u32[]{:S(2)}, u32[]{:S(2)}) collective-permute-start(bf16[4,8,1920]{2,1,0:T(8,128)(2,1)S(1)} %get-tuple-element.44), channel_id=1, source_target_pairs={{0,3},{1,0},{2,1},{3,2},{4,7},{5,4},{6,5},{7,6},{8,11},{9,8},{10,9... | collective-permute-start | bytes 368648 | tf_op jit(solution)/shard_map/ppermute | solution.py:27
  107.9 15.5 %collective-permute-start.27 = (bf16[4,8,1920]{2,1,0:T(8,128)(2,1)S(1)}, bf16[4,8,1920]{2,1,0:T(8,128)(2,1)S(1)}, u32[]{:S(2)}, u32[]{:S(2)}) collective-permute-start(bf16[4,8,1920]{2,1,0:T(8,128)(2,1)S(1)} %get-tuple-element.45), channel_id=1, source_target_pairs={{0,2},{1,3},{2,0},{3,1},{4,6},{5,7},{6,4},{7,5},{8,10},{9,11},{10,... | collective-permute-start | bytes 368648 | tf_op jit(solution)/shard_map/ppermute | solution.py:27
  109.0 14.4 %collective-permute-start.26 = (bf16[4,8,1920]{2,1,0:T(8,128)(2,1)S(1)}, bf16[4,8,1920]{2,1,0:T(8,128)(2,1)S(1)}, u32[]{:S(2)}, u32[]{:S(2)}) collective-permute-start(bf16[4,8,1920]{2,1,0:T(8,128)(2,1)S(1)} %get-tuple-element.43), channel_id=1, source_target_pairs={{0,1},{1,2},{2,3},{3,0},{4,5},{5,6},{6,7},{7,4},{8,9},{9,10},{10,1... | collective-permute-start | bytes 368648 | tf_op jit(solution)/shard_map/ppermute | solution.py:27
  119.9 7.7 %collective-permute-start.22 = (bf16[4,8,3712]{2,1,0:T(8,128)(2,1)S(1)}, bf16[4,8,3712]{2,1,0:T(8,128)(2,1)S(1)}, u32[]{:S(2)}, u32[]{:S(2)}) collective-permute-start(bf16[4,8,3712]{2,1,0:T(8,128)(2,1)S(1)} %get-tuple-element.37), channel_id=1, source_target_pairs={{0,12},{1,13},{2,14},{3,15},{4,0},{5,1},{6,2},{7,3},{8,4},{9,5},{1... | collective-permute-start | bytes 712712 | tf_op jit(solution)/shard_map/ppermute | solution.py:27
  122.0 6.6 %collective-permute-start.21 = (bf16[4,8,3712]{2,1,0:T(8,128)(2,1)S(1)}, bf16[4,8,3712]{2,1,0:T(8,128)(2,1)S(1)}, u32[]{:S(2)}, u32[]{:S(2)}) collective-permute-start(bf16[4,8,3712]{2,1,0:T(8,128)(2,1)S(1)} %get-tuple-element.38), channel_id=1, source_target_pairs={{0,8},{1,9},{2,10},{3,11},{4,12},{5,13},{6,14},{7,15},{8,0},{9,1},... | collective-permute-start | bytes 712712 | tf_op jit(solution)/shard_map/ppermute | solution.py:27
  123.1 8.2 %collective-permute-start.20 = (bf16[4,8,3712]{2,1,0:T(8,128)(2,1)S(1)}, bf16[4,8,3712]{2,1,0:T(8,128)(2,1)S(1)}, u32[]{:S(2)}, u32[]{:S(2)}) collective-permute-start(bf16[4,8,3712]{2,1,0:T(8,128)(2,1)S(1)} %get-tuple-element.36), channel_id=1, source_target_pairs={{0,4},{1,5},{2,6},{3,7},{4,8},{5,9},{6,10},{7,11},{8,12},{9,13},{1... | collective-permute-start | bytes 712712 | tf_op jit(solution)/shard_map/ppermute | solution.py:27
  131.5 8.1 %collective-permute-start.31 = (bf16[8,5632]{1,0:T(8,128)(2,1)S(1)}, bf16[8,5632]{1,0:T(8,128)(2,1)S(1)}, u32[]{:S(2)}, u32[]{:S(2)}) collective-permute-start(bf16[8,5632]{1,0:T(8,128)(2,1)S(1)} %get-tuple-element.51), channel_id=1, source_target_pairs={{0,48},{1,49},{2,50},{3,51},{4,52},{5,53},{6,54},{7,55},{8,56},{9,... | collective-permute-start | bytes 270344 | tf_op jit(solution)/shard_map/ppermute | solution.py:27
  137.2 5.0 %collective-permute-start.30 = (bf16[8,5632]{1,0:T(8,128)(2,1)S(1)}, bf16[8,5632]{1,0:T(8,128)(2,1)S(1)}, u32[]{:S(2)}, u32[]{:S(2)}) collective-permute-start(bf16[8,5632]{1,0:T(8,128)(2,1)S(1)} %get-tuple-element.52), channel_id=1, source_target_pairs={{0,32},{1,33},{2,34},{3,35},{4,36},{5,37},{6,38},{7,39},{8,40},{9,... | collective-permute-start | bytes 270344 | tf_op jit(solution)/shard_map/ppermute | solution.py:27
  137.2 5.6 %collective-permute-start.29 = (bf16[8,5632]{1,0:T(8,128)(2,1)S(1)}, bf16[8,5632]{1,0:T(8,128)(2,1)S(1)}, u32[]{:S(2)}, u32[]{:S(2)}) collective-permute-start(bf16[8,5632]{1,0:T(8,128)(2,1)S(1)} %get-tuple-element.50), channel_id=1, source_target_pairs={{0,16},{1,17},{2,18},{3,19},{4,20},{5,21},{6,22},{7,23},{8,24},{9,... | collective-permute-start | bytes 270344 | tf_op jit(solution)/shard_map/ppermute | solution.py:27
  143.5 5.2 %collective-permute-start.34 = (bf16[8,4608]{1,0:T(8,128)(2,1)S(1)}, bf16[8,4608]{1,0:T(8,128)(2,1)S(1)}, u32[]{:S(2)}, u32[]{:S(2)}) collective-permute-start(bf16[8,4608]{1,0:T(8,128)(2,1)S(1)} %get-tuple-element.55), channel_id=1, source_target_pairs={{0,16},{1,17},{2,18},{3,19},{4,20},{5,21},{6,22},{7,23},{8,24},{9,... | collective-permute-start | bytes 221192 | tf_op jit(solution)/shard_map/ppermute | solution.py:27
  143.5 5.2 %collective-permute-start.33 = (bf16[8,4608]{1,0:T(8,128)(2,1)S(1)}, bf16[8,4608]{1,0:T(8,128)(2,1)S(1)}, u32[]{:S(2)}, u32[]{:S(2)}) collective-permute-start(bf16[8,4608]{1,0:T(8,128)(2,1)S(1)} %get-tuple-element.55), channel_id=1, source_target_pairs={{0,32},{1,33},{2,34},{3,35},{4,36},{5,37},{6,38},{7,39},{8,40},{9,... | collective-permute-start | bytes 221192 | tf_op jit(solution)/shard_map/ppermute | solution.py:27
  145.3 4.0 %collective-permute-start.32 = (bf16[8,4608]{1,0:T(8,128)(2,1)S(1)}, bf16[8,4608]{1,0:T(8,128)(2,1)S(1)}, u32[]{:S(2)}, u32[]{:S(2)}) collective-permute-start(bf16[8,4608]{1,0:T(8,128)(2,1)S(1)} %get-tuple-element.55), channel_id=1, source_target_pairs={{0,48},{1,49},{2,50},{3,51},{4,52},{5,53},{6,54},{7,55},{8,56},{9,... | collective-permute-start | bytes 221192 | tf_op jit(solution)/shard_map/ppermute | solution.py:27
  149.3 7.0 %collective-permute-start.43 = (bf16[4,8,1536]{2,1,0:T(8,128)(2,1)S(1)}, bf16[4,8,1536]{2,1,0:T(8,128)(2,1)S(1)}, u32[]{:S(2)}, u32[]{:S(2)}) collective-permute-start(bf16[4,8,1536]{2,1,0:T(8,128)(2,1)S(1)} %pad_maximum_fusion.32), channel_id=1, source_target_pairs={{0,1},{1,2},{2,3},{3,0},{4,5},{5,6},{6,7},{7,4},{8,9},{9,10},{10,1... | collective-permute-start | bytes 294920 | tf_op jit(solution)/shard_map/ppermute | solution.py:27
  149.6 7.6 %collective-permute-start.42 = (bf16[4,8,1536]{2,1,0:T(8,128)(2,1)S(1)}, bf16[4,8,1536]{2,1,0:T(8,128)(2,1)S(1)}, u32[]{:S(2)}, u32[]{:S(2)}) collective-permute-start(bf16[4,8,1536]{2,1,0:T(8,128)(2,1)S(1)} %pad_maximum_fusion.32), channel_id=1, source_target_pairs={{0,2},{1,3},{2,0},{3,1},{4,6},{5,7},{6,4},{7,5},{8,10},{9,11},{10,... | collective-permute-start | bytes 294920 | tf_op jit(solution)/shard_map/ppermute | solution.py:27
  151.6 5.5 %collective-permute-start.41 = (bf16[4,8,1536]{2,1,0:T(8,128)(2,1)S(1)}, bf16[4,8,1536]{2,1,0:T(8,128)(2,1)S(1)}, u32[]{:S(2)}, u32[]{:S(2)}) collective-permute-start(bf16[4,8,1536]{2,1,0:T(8,128)(2,1)S(1)} %pad_maximum_fusion.32), channel_id=1, source_target_pairs={{0,3},{1,0},{2,1},{3,2},{4,7},{5,4},{6,5},{7,6},{8,11},{9,8},{10,9... | collective-permute-start | bytes 294920 | tf_op jit(solution)/shard_map/ppermute | solution.py:27
  152.9 7.9 %collective-permute-start.37 = (bf16[4,8,3072]{2,1,0:T(8,128)(2,1)S(1)}, bf16[4,8,3072]{2,1,0:T(8,128)(2,1)S(1)}, u32[]{:S(2)}, u32[]{:S(2)}) collective-permute-start(bf16[4,8,3072]{2,1,0:T(8,128)(2,1)S(1)} %get-tuple-element.54), channel_id=1, source_target_pairs={{0,4},{1,5},{2,6},{3,7},{4,8},{5,9},{6,10},{7,11},{8,12},{9,13},{1... | collective-permute-start | bytes 589832 | tf_op jit(solution)/shard_map/ppermute | solution.py:27
  153.0 7.8 %collective-permute-start.36 = (bf16[4,8,3072]{2,1,0:T(8,128)(2,1)S(1)}, bf16[4,8,3072]{2,1,0:T(8,128)(2,1)S(1)}, u32[]{:S(2)}, u32[]{:S(2)}) collective-permute-start(bf16[4,8,3072]{2,1,0:T(8,128)(2,1)S(1)} %get-tuple-element.54), channel_id=1, source_target_pairs={{0,8},{1,9},{2,10},{3,11},{4,12},{5,13},{6,14},{7,15},{8,0},{9,1},... | collective-permute-start | bytes 589832 | tf_op jit(solution)/shard_map/ppermute | solution.py:27
  156.3 5.1 %collective-permute-start.35 = (bf16[4,8,3072]{2,1,0:T(8,128)(2,1)S(1)}, bf16[4,8,3072]{2,1,0:T(8,128)(2,1)S(1)}, u32[]{:S(2)}, u32[]{:S(2)}) collective-permute-start(bf16[4,8,3072]{2,1,0:T(8,128)(2,1)S(1)} %get-tuple-element.54), channel_id=1, source_target_pairs={{0,12},{1,13},{2,14},{3,15},{4,0},{5,1},{6,2},{7,3},{8,4},{9,5},{1... | collective-permute-start | bytes 589832 | tf_op jit(solution)/shard_map/ppermute | solution.py:27
  157.3 10.0 %collective-permute-start.46 = (bf16[4,4,8,1536]{3,2,1,0:T(8,128)(2,1)S(1)}, bf16[4,4,8,1536]{3,2,1,0:T(8,128)(2,1)S(1)}, u32[]{:S(2)}, u32[]{:S(2)}) collective-permute-start(bf16[4,4,8,1536]{3,2,1,0:T(8,128)(2,1)S(1)} %get-tuple-element.49), channel_id=1, source_target_pairs={{0,4},{1,5},{2,6},{3,7},{4,8},{5,9},{6,10},{7,11},{8,12},{9,13},{1... | collective-permute-start | bytes 1179656 | tf_op jit(solution)/shard_map/ppermute | solution.py:27
  161.6 20.8 %collective-permute-start.40 = (bf16[4,4,8,3072]{3,2,1,0:T(8,128)(2,1)S(1)}, bf16[4,4,8,3072]{3,2,1,0:T(8,128)(2,1)S(1)}, u32[]{:S(2)}, u32[]{:S(2)}) collective-permute-start(bf16[4,4,8,3072]{3,2,1,0:T(8,128)(2,1)S(1)} %get-tuple-element.40), channel_id=1, source_target_pairs={{0,1},{1,2},{2,3},{3,0},{4,5},{5,6},{6,7},{7,4},{8,9},{9,10},{10,1... | collective-permute-start | bytes 2359304 | tf_op jit(solution)/shard_map/ppermute | solution.py:27
  162.2 20.2 %collective-permute-start.39 = (bf16[4,4,8,3072]{3,2,1,0:T(8,128)(2,1)S(1)}, bf16[4,4,8,3072]{3,2,1,0:T(8,128)(2,1)S(1)}, u32[]{:S(2)}, u32[]{:S(2)}) collective-permute-start(bf16[4,4,8,3072]{3,2,1,0:T(8,128)(2,1)S(1)} %get-tuple-element.40), channel_id=1, source_target_pairs={{0,2},{1,3},{2,0},{3,1},{4,6},{5,7},{6,4},{7,5},{8,10},{9,11},{10,... | collective-permute-start | bytes 2359304 | tf_op jit(solution)/shard_map/ppermute | solution.py:27
  163.8 19.2 %collective-permute-start.38 = (bf16[4,4,8,3072]{3,2,1,0:T(8,128)(2,1)S(1)}, bf16[4,4,8,3072]{3,2,1,0:T(8,128)(2,1)S(1)}, u32[]{:S(2)}, u32[]{:S(2)}) collective-permute-start(bf16[4,4,8,3072]{3,2,1,0:T(8,128)(2,1)S(1)} %get-tuple-element.40), channel_id=1, source_target_pairs={{0,3},{1,0},{2,1},{3,2},{4,7},{5,4},{6,5},{7,6},{8,11},{9,8},{10,9... | collective-permute-start | bytes 2359304 | tf_op jit(solution)/shard_map/ppermute | solution.py:27
  165.8 8.7 %collective-permute-start.45 = (bf16[4,4,8,1536]{3,2,1,0:T(8,128)(2,1)S(1)}, bf16[4,4,8,1536]{3,2,1,0:T(8,128)(2,1)S(1)}, u32[]{:S(2)}, u32[]{:S(2)}) collective-permute-start(bf16[4,4,8,1536]{3,2,1,0:T(8,128)(2,1)S(1)} %get-tuple-element.49), channel_id=1, source_target_pairs={{0,8},{1,9},{2,10},{3,11},{4,12},{5,13},{6,14},{7,15},{8,0},{9,1},... | collective-permute-start | bytes 1179656 | tf_op jit(solution)/shard_map/ppermute | solution.py:27
  167.2 14.1 %collective-permute-start.44 = (bf16[4,4,8,1536]{3,2,1,0:T(8,128)(2,1)S(1)}, bf16[4,4,8,1536]{3,2,1,0:T(8,128)(2,1)S(1)}, u32[]{:S(2)}, u32[]{:S(2)}) collective-permute-start(bf16[4,4,8,1536]{3,2,1,0:T(8,128)(2,1)S(1)} %get-tuple-element.49), channel_id=1, source_target_pairs={{0,12},{1,13},{2,14},{3,15},{4,0},{5,1},{6,2},{7,3},{8,4},{9,5},{1... | collective-permute-start | bytes 1179656 | tf_op jit(solution)/shard_map/ppermute | solution.py:27
  186.1 31.9 %collective-permute-start.47 = (f32[512,512]{1,0:T(8,128)S(1)}, f32[512,512]{1,0:T(8,128)S(1)}, u32[]{:S(2)}, u32[]{:S(2)}) collective-permute-start(f32[512,512]{1,0:T(8,128)S(1)} %fusion.12), channel_id=1, source_target_pairs={{64,0},{65,1},{66,2},{67,3},{68,4},{69,5},{70,6},{71,7},{72,8},{73... | collective-permute-start | bytes 3145736 | tf_op jit(solution)/shard_map/ppermute | solution.py:78
  210.9 16.1 %collective-permute-start.48 = (bf16[512,2304]{1,0:T(8,128)(2,1)S(1)}, bf16[512,2304]{1,0:T(8,128)(2,1)S(1)}, u32[]{:S(2)}, u32[]{:S(2)}) collective-permute-start(bf16[512,2304]{1,0:T(8,128)(2,1)S(1)} %slice.177), channel_id=1, source_target_pairs={{64,0},{65,1},{66,2},{67,3},{68,4},{69,5},{70,6},{71,7},{72,8},{73... | collective-permute-start | bytes 7077896 | tf_op jit(solution)/shard_map/ppermute | solution.py:78
  (16 other events, 100.4 us)
